TPU v7x, 32 devices: a whole 2x2x4 slice. The times are simulated.
32 devices in a mesh: dp: 4 (over y, x), vocab: 8 (over z, core).
Axes of the slice: x: 2, y: 2, z: 4, core: 2. Of those that a mesh axis runs over, the one named last changes fastest.
Arguments:
- hidden: bfloat16 [128, 3584], P(('dp', 'vocab')), may hold values from -6 to 6
- head_weight: bfloat16 [3584, 256000], P(None, ('dp', 'vocab')), may hold values from -0.75 to 0.75
- teacher_ids: int32 [128, 128], P(('dp', 'vocab')), may hold values from 0 to 255999
- teacher_probs: float32 [128, 128], P(('dp', 'vocab')), may hold values from 0.0001 to 0.015
- target_ids: int32 [128], P(('dp', 'vocab')), may hold values from 0 to 255999
Outputs:
- token_loss: float32 [128], P(('dp', 'vocab'))
- hidden_grad: bfloat16 [128, 3584], P(('dp', 'vocab'))
All inputs are finite; a program needn't handle non-finite values.
Results may differ from a plain program's by a relative error of at most 0.004.
Values may be sent and summed in bfloat16 or wider, within the bound.
A program may use at most 128 MiB of HBM per device.

v0:
```python
import jax
import jax.numpy as jnp
from jax import lax
from jax.sharding import PartitionSpec as P

SOFT_CAP = 30.0
CE_WEIGHT = 0.5
LOSS_SCALE = 8.0
BLOCK_ROWS = 32


def sparse_rows(teacher_ids, teacher_probs, columns):
    token_count, kept = teacher_ids.shape
    block_rows = BLOCK_ROWS
    id_blocks = teacher_ids.reshape(token_count // block_rows, block_rows, kept)
    prob_blocks = teacher_probs.reshape(token_count // block_rows, block_rows, kept)

    def one_block(pair):
        id_rows, prob_rows = pair
        match = id_rows[:, :, None] == columns[None, None, :]
        return jnp.sum(jnp.where(match, prob_rows[:, :, None], 0.0), axis=1)

    summed = lax.map(one_block, (id_blocks, prob_blocks))
    return summed.reshape(token_count, columns.shape[0])


def per_device(hidden, head_weight, teacher_ids, teacher_probs, target_ids):
    slice_width = head_weight.shape[1]
    tokens_local = hidden.shape[0]
    position = lax.axis_index(("dp", "vocab"))
    first_column = position * slice_width
    columns = first_column + jnp.arange(slice_width, dtype=jnp.int32)
    raw_logits = jnp.dot(
        lax.all_gather(hidden, ("dp", "vocab"), axis=0, tiled=True),
        head_weight,
        preferred_element_type=jnp.float32,
    )
    capped = SOFT_CAP * jnp.tanh(raw_logits / SOFT_CAP)
    all_ids, all_targets = (
        lax.all_gather(teacher_ids, ("dp", "vocab"), axis=0, tiled=True),
        lax.all_gather(target_ids, ("dp", "vocab"), axis=0, tiled=True),
    )
    all_probs = lax.all_gather(teacher_probs, ("dp", "vocab"), axis=0, tiled=True)
    sparse = sparse_rows(all_ids, all_probs, columns)
    target_hit = columns[None, :] == all_targets[:, None]
    part_dot = jnp.sum(capped * sparse, axis=1)
    part_target = jnp.sum(jnp.where(target_hit, capped, 0.0), axis=1)
    part_exp = jnp.sum(jnp.exp(capped), axis=1)
    exp_sum, teacher_dot, target_logit = lax.psum(
        (part_exp, part_dot, part_target), ("dp", "vocab")
    )
    log_total = jnp.log(exp_sum)
    teacher_sum = jnp.sum(all_probs, axis=1)
    every_loss = (
        jnp.sum(all_probs * jnp.log(all_probs), axis=1)
        - teacher_dot
        + teacher_sum * log_total
        + CE_WEIGHT * (log_total - target_logit)
    )
    token_loss = lax.dynamic_slice_in_dim(every_loss, position * tokens_local, tokens_local)
    softmax_rows = jnp.exp(capped - log_total[:, None])
    onehot = jnp.where(target_hit, 1.0, 0.0)
    raw_grads = LOSS_SCALE * (
        (teacher_sum + CE_WEIGHT)[:, None] * softmax_rows - sparse - CE_WEIGHT * onehot
    )
    grads = (raw_grads * (1.0 - (capped / SOFT_CAP) ** 2)).astype(jnp.bfloat16)
    summed = lax.psum_scatter(
        jnp.einsum("tv,dv->td", grads, head_weight, preferred_element_type=jnp.float32),
        ("dp", "vocab"),
        scatter_dimension=0,
        tiled=True,
    )
    return (token_loss, summed.astype(jnp.bfloat16))


def solution(mesh):
    in_specs = (
        P(("dp", "vocab"), None),
        P(None, ("dp", "vocab")),
        P(("dp", "vocab"), None),
        P(("dp", "vocab"), None),
        P(("dp", "vocab")),
    )
    out_specs = (P(("dp", "vocab")), P(("dp", "vocab"), None))
    return jax.shard_map(
        per_device, mesh=mesh, in_specs=in_specs, out_specs=out_specs, check_vma=False
    )
```

profile of v0, /device:TPU:0, one launch (start us, length us, event | category | flops | bytes accessed | tf_op | source)
XLA Modules:
  0.0 491.0 jit_solution(7940874425076551939)
XLA Ops:
  0.6 0.9 dynamic-update-slice
  1.5 42.0 %all-reduce = s32[128]{0:T(128)S(1)} all-reduce(s32[128]{0:T(128)S(1)} %dynamic-update-slice), channel_id=1, replica_groups=mesh['dp'=4,'vocab'=8] {'dp','vocab'}, use_global_device_ids=true, to_apply=%add | all-reduce | flops 128 | bytes 1024
  43.5 40.7 %all-gather.2 = s32[32,4,128]{2,1,0:T(4,128)S(1)} all-gather(s32[1,4,128]{2,1,0:T(4,128)} %bitcast.28), channel_id=1, replica_groups=mesh['dp'=4,'vocab'=8] {'dp','vocab'}, dimensions={0}, use_global_device_ids=true | all-gather | bytes 67584 | tf_op jit(solution)/shard_map/all_gather | solution.py:40
  84.2 37.1 %all-gather = f32[32,4,128]{2,1,0:T(4,128)S(1)} all-gather(f32[1,4,128]{2,1,0:T(4,128)} %bitcast.29), channel_id=1, replica_groups=mesh['dp'=4,'vocab'=8] {'dp','vocab'}, dimensions={0}, use_global_device_ids=true | all-gather | bytes 67584 | tf_op jit(solution)/shard_map/all_gather | solution.py:43
  121.3 171.5 %while.11 = (s32[]{:T(128)}, f32[4,32,8000]{2,1,0:T(8,128)}, s32[4,32,128]{2,1,0:T(8,128)S(1)}, f32[4,32,128]{2,1,0:T(8,128)S(1)}, s32[]{:T(128)}, /*index=5*/s32[]{:T(128)}) while((s32[]{:T(128)}, f32[4,32,8000]{2,1,0:T(8,128)}, s32[4,32,128]{2,1,0:T(8,128)S(1)}, f32[4,32,128]{2,1,0:T(8,128)S(1)}, s32[]{:T(128)}, ...), condition=%wide.region_3.4_spmd.clone, body=%wide.region_1.3_spmd.clone.sunk | while | flops 98056000 | bytes 3242589 | solution.py:23
  121.3 41.8 %select_reduce_fusion.2 = f32[32,8000]{1,0:T(8,128)S(1)} fusion(f32[32,128]{1,0:T(8,128)S(1)} %dynamic-slice_bitcast_fusion.4, s32[32,128]{1,0:T(8,128)S(1)} %dynamic-slice_bitcast_fusion.5, s32[8000]{0:T(1024)S(1)} %iota_add_fusion.3), kind=kLoop, calls=%fused_computation.1.clone.1 | loop fusion | flops 98048000 | bytes 1088768 | tf_op jit(solution)/shard_map/while/body/eval_jaxpr/reduce_sum | solution.py:21
  163.1 1.1 bitcast_dynamic-update-slice_fusion.2
  164.1 41.8 %select_reduce_fusion.2 = f32[32,8000]{1,0:T(8,128)S(1)} fusion(f32[32,128]{1,0:T(8,128)S(1)} %dynamic-slice_bitcast_fusion.4, s32[32,128]{1,0:T(8,128)S(1)} %dynamic-slice_bitcast_fusion.5, s32[8000]{0:T(1024)S(1)} %iota_add_fusion.3), kind=kLoop, calls=%fused_computation.1.clone.1 | loop fusion | flops 98048000 | bytes 1088768 | tf_op jit(solution)/shard_map/while/body/eval_jaxpr/reduce_sum | solution.py:21
  205.9 1.1 bitcast_dynamic-update-slice_fusion.2
  207.0 41.8 %select_reduce_fusion.2 = f32[32,8000]{1,0:T(8,128)S(1)} fusion(f32[32,128]{1,0:T(8,128)S(1)} %dynamic-slice_bitcast_fusion.4, s32[32,128]{1,0:T(8,128)S(1)} %dynamic-slice_bitcast_fusion.5, s32[8000]{0:T(1024)S(1)} %iota_add_fusion.3), kind=kLoop, calls=%fused_computation.1.clone.1 | loop fusion | flops 98048000 | bytes 1088768 | tf_op jit(solution)/shard_map/while/body/eval_jaxpr/reduce_sum | solution.py:21
  248.8 1.0 bitcast_dynamic-update-slice_fusion.2
  249.9 41.8 %select_reduce_fusion.2 = f32[32,8000]{1,0:T(8,128)S(1)} fusion(f32[32,128]{1,0:T(8,128)S(1)} %dynamic-slice_bitcast_fusion.4, s32[32,128]{1,0:T(8,128)S(1)} %dynamic-slice_bitcast_fusion.5, s32[8000]{0:T(1024)S(1)} %iota_add_fusion.3), kind=kLoop, calls=%fused_computation.1.clone.1 | loop fusion | flops 98048000 | bytes 1088768 | tf_op jit(solution)/shard_map/while/body/eval_jaxpr/reduce_sum | solution.py:21
  291.7 1.0 bitcast_dynamic-update-slice_fusion.2
  292.7 0.0 copy-start
  292.7 5.6 %copy.12 = f32[128,8000]{0,1:T(8,128)} copy(f32[128,8000]{1,0:T(8,128)} %bitcast.22) | data formatting | bytes 8192000 | tf_op jit(solution)/shard_map/reshape | solution.py:24
  298.4 0.0 copy-done
  298.4 41.8 %all-gather.1 = bf16[32,4,3584]{2,1,0:T(4,128)(2,1)S(1)} all-gather(bf16[1,4,3584]{2,1,0:T(4,128)(2,1)S(1)} %bitcast.27), channel_id=1, replica_groups=mesh['dp'=4,'vocab'=8] {'dp','vocab'}, dimensions={0}, use_global_device_ids=true | all-gather | bytes 946176 | tf_op jit(solution)/shard_map/all_gather | solution.py:34
  340.2 0.2 reshape.35
  340.4 25.1 %exponential_reduce_fusion = (f32[128]{0:T(128)S(1)}, f32[128]{0:T(128)S(1)}, f32[128]{0:T(128)S(1)}, f32[128,8000]{0,1:T(8,128)}) fusion(s32[128]{0:T(128)S(1)} %all-reduce, s32[8000]{0:T(1024)S(1)} %iota_add_fusion.1, f32[128,8000]{0,1:T(8,128)} %copy.12, bf16[128,3584]{1,0:T(8,128)(2,1)S(1)} %reshape.35, bf16[3584,8000]{0,1:T(8,128)(2,1)} %param.8), kind=kOutput, calls=%fused_computation.16 | convolution fusion | flops 7348224000 | bytes 66487552 | tf_op jit(solution)/shard_map/dot_general | solution.py:33
  365.6 37.9 %psum.22 = f32[128]{0:T(128)S(1)} all-reduce(f32[128]{0:T(128)S(1)} %get-tuple-element.43), channel_id=1, replica_groups=mesh['dp'=4,'vocab'=8] {'dp','vocab'}, use_global_device_ids=true, to_apply=%region_8.9 | all-reduce | flops 128 | bytes 1024 | tf_op jit(solution)/shard_map/psum | solution.py:49
  403.4 0.1 reduce
  403.5 0.1 reshape.38
  403.7 23.4 %fusion.9 = f32[128,3584]{1,0:T(8,128)S(1)} fusion(bf16[3584,8000]{0,1:T(8,128)(2,1)} %param.8, f32[128,8000]{0,1:T(8,128)} %get-tuple-element.59, f32[128,8000]{0,1:T(8,128)} %copy.12, f32[128]{0:T(128)S(1)} %log.7, f32[128]{0:T(128)S(1)} %broadcast_add_fusion, s32[128]{0:T(128)S(1)} %all-reduce, s32[8000]{0:T(1024)S(1)} %iota_add_fusion.1), kind=kOutput, calls=%fused_computation.18 | convolution fusion | flops 7353344000 | bytes 67404544 | tf_op jit(solution)/shard_map/tv,dv->td/dot_general | solution.py:68
  427.1 62.6 %all-reduce.4 = (f32[128]{0:T(128)S(1)}, f32[128]{0:T(128)S(1)}, bf16[128,3584]{1,0:T(8,128)(2,1)S(1)}) all-reduce(f32[128]{0:T(128)S(1)} %get-tuple-element.44, f32[128]{0:T(128)S(1)} %get-tuple-element.45, f32[128,3584]{1,0:T(8,128)S(1)} %fusion.9), channel_id=1, replica_groups=mesh['dp'=4,'vocab'=8] {'dp','vocab'}, use_global_device_ids=true, to_apply=%region_10.11 | all-reduce | flops 459008 | bytes 2754560 | tf_op jit(solution)/shard_map/psum | solution.py:49
  489.7 0.1 fusion.20
  489.8 0.6 dynamic_slice.11
  490.4 0.6 dynamic-slice_convert_fusion
  (18 shorter events, 0.1 us)
Async XLA Ops:
  292.7 5.6 %copy-start = (bf16[4,3584]{1,0:T(4,128)(2,1)S(1)}, bf16[4,3584]{1,0:T(4,128)(2,1)}, u32[]{:S(2)}) copy-start(bf16[4,3584]{1,0:T(4,128)(2,1)} %param.7) | copy-start | bytes 86020
where the time goes:
time: 492 us; the launch traced here: 491 us
  blocking collectives  262 us (53%)
  other arithmetic  167 us (34%)
  matrix products  48.5 us (10%)
  local copies, waits for them, and re-layouts  12.3 us (2%)
    reduce_sum x4, other arithmetic, one_block(): return jnp.sum(jnp.where(match, prob_rows[:, :, None], 0.0), axis=1)  167 us
    psum x2, blocking collectives, per_device(): lax.psum((part_exp, part_dot, part_target), ('dp', 'vocab'))  100 us
    unnamed x1, blocking collectives  42 us
    all_gather x1, blocking collectives, per_device(): lax.all_gather(hidden, ('dp', 'vocab'), axis=0, tiled=True)  41.8 us
    all_gather x1, blocking collectives, per_device(): lax.all_gather(teacher_ids, ('dp', 'vocab'), axis=0, tiled=True)  40.7 us
    all_gather x1, blocking collectives, per_device(): lax.all_gather(teacher_probs, ('dp', 'vocab'), axis=0, tiled=True)  37.1 us
    dot_general x1, matrix products, per_device(): jnp.dot(lax.all_gather(hidden, ('dp', 'vocab'), axis=0, tiled=True), head...  25.1 us
    dot_general x1, matrix products, per_device(): jnp.einsum('tv,dv->td', grads, head_weight, preferred_element_type=jnp.fl...  23.4 us

commit v1 on v0

--- a/solution.py
+++ b/solution.py
@@ -47,7 +47,7 @@
     part_target = jnp.sum(jnp.where(target_hit, capped, 0.0), axis=1)
     part_exp = jnp.sum(jnp.exp(capped), axis=1)
     exp_sum, teacher_dot, target_logit = lax.psum(
-        (part_exp, part_dot, part_target), ("dp", "vocab")
+        lax.psum((part_exp, part_dot, part_target), "vocab"), "dp"
     )
     log_total = jnp.log(exp_sum)
     teacher_sum = jnp.sum(all_probs, axis=1)

time: 492 us -> 472 us (0.959)
  blocking collectives: 262 us -> 242 us
    psum x2, blocking collectives: 100 us -> 23.4 us  [the longest x1 13.9 us: per_device(): lax.psum((part_exp, part_dot, part_target), 'vocab')]
    unnamed x1 -> x2, blocking collectives: 42 us -> 93.9 us
    all_gather x1, blocking collectives: 37.1 us -> 43.7 us  [per_device(): lax.all_gather(teacher_probs, ('dp', 'vocab'), axis=0, tiled=True)]
where the time goes in v1:
time: 472 us; the launch traced here: 471 us
  blocking collectives  242 us (51%)
  other arithmetic  167 us (35%)
  matrix products  48.5 us (10%)
  local copies, waits for them, and re-layouts  12.3 us (3%)
    reduce_sum x4, other arithmetic, one_block(): return jnp.sum(jnp.where(match, prob_rows[:, :, None], 0.0), axis=1)  167 us
    unnamed x2, blocking collectives  93.9 us
    all_gather x1, blocking collectives, per_device(): lax.all_gather(teacher_probs, ('dp', 'vocab'), axis=0, tiled=True)  43.7 us
    all_gather x1, blocking collectives, per_device(): lax.all_gather(teacher_ids, ('dp', 'vocab'), axis=0, tiled=True)  40.7 us
    all_gather x1, blocking collectives, per_device(): lax.all_gather(hidden, ('dp', 'vocab'), axis=0, tiled=True)  40.6 us
    dot_general x1, matrix products, per_device(): jnp.dot(lax.all_gather(hidden, ('dp', 'vocab'), axis=0, tiled=True), head...  25.2 us
    dot_general x1, matrix products, per_device(): jnp.einsum('tv,dv->td', grads, head_weight, preferred_element_type=jnp.fl...  23.4 us
    psum x1, blocking collectives, per_device(): lax.psum((part_exp, part_dot, part_target), 'vocab')  13.9 us

profile of v1, /device:TPU:0, one launch (start us, length us, event | category | flops | bytes accessed | tf_op | source)
XLA Modules:
  0.0 471.4 jit_solution(6494786810547052619)
XLA Ops:
  0.6 43.7 %all-gather = f32[32,4,128]{2,1,0:T(4,128)S(1)} all-gather(f32[1,4,128]{2,1,0:T(4,128)} %bitcast.27), channel_id=1, replica_groups=mesh['dp'=4,'vocab'=8] {'dp','vocab'}, dimensions={0}, use_global_device_ids=true | all-gather | bytes 67584 | tf_op jit(solution)/shard_map/all_gather | solution.py:43
  44.3 0.1 reduce
  44.5 0.1 reshape.38
  44.6 0.9 dynamic-update-slice
  45.4 36.9 %all-reduce = s32[128]{0:T(128)S(1)} all-reduce(s32[128]{0:T(128)S(1)} %dynamic-update-slice), channel_id=1, replica_groups=mesh['dp'=4,'vocab'=8] {'dp','vocab'}, use_global_device_ids=true, to_apply=%add | all-reduce | flops 128 | bytes 1024
  82.3 40.7 %all-gather.2 = s32[32,4,128]{2,1,0:T(4,128)S(1)} all-gather(s32[1,4,128]{2,1,0:T(4,128)} %bitcast.28), channel_id=1, replica_groups=mesh['dp'=4,'vocab'=8] {'dp','vocab'}, dimensions={0}, use_global_device_ids=true | all-gather | bytes 67584 | tf_op jit(solution)/shard_map/all_gather | solution.py:40
  123.0 171.5 %while.11 = (s32[]{:T(128)}, f32[4,32,8000]{2,1,0:T(8,128)}, s32[4,32,128]{2,1,0:T(8,128)S(1)}, f32[4,32,128]{2,1,0:T(8,128)S(1)}, s32[]{:T(128)}, /*index=5*/s32[]{:T(128)}) while((s32[]{:T(128)}, f32[4,32,8000]{2,1,0:T(8,128)}, s32[4,32,128]{2,1,0:T(8,128)S(1)}, f32[4,32,128]{2,1,0:T(8,128)S(1)}, s32[]{:T(128)}, ...), condition=%wide.region_3.4_spmd.clone, body=%wide.region_1.3_spmd.clone.sunk | while | flops 98056000 | bytes 3242589 | solution.py:23
  123.1 41.8 %select_reduce_fusion.2 = f32[32,8000]{1,0:T(8,128)S(1)} fusion(f32[32,128]{1,0:T(8,128)S(1)} %dynamic-slice_bitcast_fusion.4, s32[32,128]{1,0:T(8,128)S(1)} %dynamic-slice_bitcast_fusion.5, s32[8000]{0:T(1024)S(1)} %iota_add_fusion.3), kind=kLoop, calls=%fused_computation.1.clone.1 | loop fusion | flops 98048000 | bytes 1088768 | tf_op jit(solution)/shard_map/while/body/eval_jaxpr/reduce_sum | solution.py:21
  164.9 1.1 bitcast_dynamic-update-slice_fusion.2
  165.9 41.8 %select_reduce_fusion.2 = f32[32,8000]{1,0:T(8,128)S(1)} fusion(f32[32,128]{1,0:T(8,128)S(1)} %dynamic-slice_bitcast_fusion.4, s32[32,128]{1,0:T(8,128)S(1)} %dynamic-slice_bitcast_fusion.5, s32[8000]{0:T(1024)S(1)} %iota_add_fusion.3), kind=kLoop, calls=%fused_computation.1.clone.1 | loop fusion | flops 98048000 | bytes 1088768 | tf_op jit(solution)/shard_map/while/body/eval_jaxpr/reduce_sum | solution.py:21
  207.7 1.1 bitcast_dynamic-update-slice_fusion.2
  208.8 41.8 %select_reduce_fusion.2 = f32[32,8000]{1,0:T(8,128)S(1)} fusion(f32[32,128]{1,0:T(8,128)S(1)} %dynamic-slice_bitcast_fusion.4, s32[32,128]{1,0:T(8,128)S(1)} %dynamic-slice_bitcast_fusion.5, s32[8000]{0:T(1024)S(1)} %iota_add_fusion.3), kind=kLoop, calls=%fused_computation.1.clone.1 | loop fusion | flops 98048000 | bytes 1088768 | tf_op jit(solution)/shard_map/while/body/eval_jaxpr/reduce_sum | solution.py:21
  250.6 1.0 bitcast_dynamic-update-slice_fusion.2
  251.7 41.8 %select_reduce_fusion.2 = f32[32,8000]{1,0:T(8,128)S(1)} fusion(f32[32,128]{1,0:T(8,128)S(1)} %dynamic-slice_bitcast_fusion.4, s32[32,128]{1,0:T(8,128)S(1)} %dynamic-slice_bitcast_fusion.5, s32[8000]{0:T(1024)S(1)} %iota_add_fusion.3), kind=kLoop, calls=%fused_computation.1.clone.1 | loop fusion | flops 98048000 | bytes 1088768 | tf_op jit(solution)/shard_map/while/body/eval_jaxpr/reduce_sum | solution.py:21
  293.5 1.0 bitcast_dynamic-update-slice_fusion.2
  294.5 0.0 copy-start
  294.5 5.6 %copy.12 = f32[128,8000]{0,1:T(8,128)} copy(f32[128,8000]{1,0:T(8,128)} %bitcast.22) | data formatting | bytes 8192000 | tf_op jit(solution)/shard_map/reshape | solution.py:24
  300.2 0.0 copy-done
  300.2 40.6 %all-gather.1 = bf16[32,4,3584]{2,1,0:T(4,128)(2,1)S(1)} all-gather(bf16[1,4,3584]{2,1,0:T(4,128)(2,1)S(1)} %bitcast.26), channel_id=1, replica_groups=mesh['dp'=4,'vocab'=8] {'dp','vocab'}, dimensions={0}, use_global_device_ids=true | all-gather | bytes 946176 | tf_op jit(solution)/shard_map/all_gather | solution.py:34
  340.8 0.2 reshape.35
  341.0 25.2 %exponential_reduce_fusion = (f32[128]{0:T(128)S(1)}, f32[128]{0:T(128)S(1)}, f32[128]{0:T(128)S(1)}, f32[128,8000]{0,1:T(8,128)}) fusion(s32[128]{0:T(128)S(1)} %all-reduce, s32[8000]{0:T(1024)S(1)} %iota_add_fusion.1, f32[128,8000]{0,1:T(8,128)} %copy.12, bf16[128,3584]{1,0:T(8,128)(2,1)S(1)} %reshape.35, bf16[3584,8000]{0,1:T(8,128)(2,1)} %param.8), kind=kOutput, calls=%fused_computation.16 | convolution fusion | flops 7348224000 | bytes 66487552 | tf_op jit(solution)/shard_map/dot_general | solution.py:33
  366.2 13.9 %all-reduce.2 = (f32[128]{0:T(128)S(1)}, f32[128]{0:T(128)S(1)}, f32[128]{0:T(128)S(1)}) all-reduce(f32[128]{0:T(128)S(1)} %get-tuple-element.44, f32[128]{0:T(128)S(1)} %get-tuple-element.45, f32[128]{0:T(128)S(1)} %get-tuple-element.43), channel_id=1, replica_groups=mesh['dp'=4,'vocab'=8] {'vocab'}, use_global_device_ids=true, to_apply=%region_12.13 | all-reduce | flops 384 | bytes 3072 | tf_op jit(solution)/shard_map/psum | solution.py:50
  380.1 9.5 %all-reduce.3 = (f32[128]{0:T(128)S(1)}, f32[128]{0:T(128)S(1)}, f32[128]{0:T(128)S(1)}) all-reduce(f32[128]{0:T(128)S(1)} %get-tuple-element.56, f32[128]{0:T(128)S(1)} %get-tuple-element.57, f32[128]{0:T(128)S(1)} %get-tuple-element.58), channel_id=1, replica_groups=mesh['dp'=4,'vocab'=8] {'dp'}, use_global_device_ids=true, to_apply=%region_13.14 | all-reduce | flops 384 | bytes 3072 | tf_op jit(solution)/shard_map/psum | solution.py:49
  389.6 0.1 fusion.20
  389.7 0.6 dynamic_slice.11
  390.3 23.4 %fusion.9 = f32[128,3584]{1,0:T(8,128)S(1)} fusion(bf16[3584,8000]{0,1:T(8,128)(2,1)} %param.8, f32[128,8000]{0,1:T(8,128)} %get-tuple-element.65, f32[128,8000]{0,1:T(8,128)} %copy.12, f32[128]{0:T(128)S(1)} %get-tuple-element.64, f32[128]{0:T(128)S(1)} %get-tuple-element.62, s32[128]{0:T(128)S(1)} %all-reduce, s32[8000]{0:T(1024)S(1)} %iota_add_fusion.1), kind=kOutput, calls=%fused_computation.18 | convolution fusion | flops 7353344000 | bytes 67404544 | tf_op jit(solution)/shard_map/tv,dv->td/dot_general | solution.py:68
  413.7 57.0 %all-reduce.5 = bf16[128,3584]{1,0:T(8,128)(2,1)S(1)} all-reduce(f32[128,3584]{1,0:T(8,128)S(1)} %fusion.9), channel_id=2, replica_groups=mesh['dp'=4,'vocab'=8] {'dp','vocab'}, use_global_device_ids=true, to_apply=%region_14.15.clone | all-reduce | flops 458752 | bytes 2752512
  470.7 0.6 dynamic-slice_convert_fusion
  (16 shorter events, 0.1 us)
Async XLA Ops:
  294.5 5.6 %copy-start = (bf16[4,3584]{1,0:T(4,128)(2,1)S(1)}, bf16[4,3584]{1,0:T(4,128)(2,1)}, u32[]{:S(2)}) copy-start(bf16[4,3584]{1,0:T(4,128)(2,1)} %param.7) | copy-start | bytes 86020
